TPU v7x, 512 devices: a whole 4x8x8 slice. The times are simulated.
512 devices in a mesh: doc: 16 (over x, z_hi), samp: 8 (over y), tok: 4 (over z_lo, core).
Axes of the slice: x: 4, y: 8, z: 8 (z_hi: 4, z_lo: 2; z = z_hi * 2 + z_lo), core: 2. Of those that a mesh axis runs over, the one named last changes fastest.
Arguments:
- context: bfloat16 [512, 128, 1024], P(('doc', 'samp', 'tok')), parts along dimension 0, may hold values from -6 to 6
- hidden: bfloat16 [512, 128, 1024], P(('doc', 'samp', 'tok')), parts along dimension 0, may hold values from -12 to 12
- out_weight: bfloat16 [1024, 1024], P(None, ('samp', 'tok')), may hold values from -0.1875 to 0.1875
- out_bias: float32 [1024], replicated, may hold values from -3 to 3
- norm_gain: float32 [1024], replicated, may hold values from 0.5 to 1.5
- norm_bias: float32 [1024], replicated, may hold values from -2 to 2
- token_ids: int32 [512, 128], P(('doc', 'samp', 'tok')), parts along dimension 0, may hold values from 0 to 50264
- lengths: int32 [512], P(('doc', 'samp', 'tok')), parts along dimension 0, may hold values from 32 to 128, as said below
- idf_table: bfloat16 [50265], replicated, may hold values from 1 to 12
Outputs:
- embeddings: bfloat16 [512, 128, 1024], P(('doc', 'samp', 'tok')), parts along dimension 0
- precision: float32 [512, 32], P(('doc', 'samp', 'tok')), parts along dimension 0
- recall: float32 [512, 32], P(('doc', 'samp', 'tok')), parts along dimension 0
- f_score: float32 [512, 32], P(('doc', 'samp', 'tok')), parts along dimension 0
- utility: float32 [512], P(('doc', 'samp', 'tok')), parts along dimension 0
There are 16 independent parts, one for each index of `doc`. A program takes and returns all parts, laid end to end along the dimension named above; an argument that names none is the same for every part. Nothing has to cross between parts.
Inputs may be any that keep to these rules, and one draw needn't show every extreme that they name: `lengths`: in every document some summary has all 128 tokens real.
All inputs are finite; a program needn't handle non-finite values.
Results may differ from a plain program's by a relative error of at most 0.001.
Values may be sent and summed in bfloat16 or wider, within the bound.
A program may use at most 64 MiB of HBM per device.

v0:
```python
import jax
import jax.numpy as jnp
from jax import lax
from jax.sharding import PartitionSpec as P


def local(
    context, hidden, out_weight, out_bias, norm_gain, norm_bias, token_ids, lengths, idf_table
):
    seq_len = context.shape[1]
    width = context.shape[2]
    group_size = lax.axis_size(("samp", "tok"))
    my_index = lax.axis_index(("samp", "tok"))
    local_ctx = context.reshape(seq_len, width)
    pre = jnp.dot(
        local_ctx,
        lax.all_gather(out_weight, ("samp", "tok"), axis=1, tiled=True),
        preferred_element_type=jnp.float32,
    )
    mixed = hidden.reshape(seq_len, width).astype(jnp.float32) + pre + out_bias
    centre = mixed - jnp.mean(mixed, axis=-1, keepdims=True)
    spread = jnp.mean(centre * centre, axis=-1, keepdims=True)
    embedded = (centre * lax.rsqrt(spread + 1e-07) * norm_gain + norm_bias).astype(jnp.bfloat16)
    values = embedded.astype(jnp.float32)
    units = (values * lax.rsqrt(jnp.sum(values * values, axis=-1, keepdims=True) + 1e-06)).astype(
        jnp.bfloat16
    )
    positions = jnp.arange(seq_len, dtype=jnp.int32)
    my_valid = positions < lengths[0]
    my_weights = jnp.where(my_valid, idf_table[token_ids[0]], jnp.zeros((), jnp.bfloat16))
    my_weights_f = my_weights.astype(jnp.float32)
    my_total = jnp.sum(my_weights_f)

    def block_scores(some_units, some_weights):
        count = some_weights.shape[0]
        flat_units = some_units.reshape(count * seq_len, width)
        sim = lax.dot_general(
            units, flat_units, (((1,), (1,)), ((), ())), preferred_element_type=jnp.float32
        )
        other_valid = (some_weights > 0).reshape(count * seq_len)
        masked = jnp.where(my_valid[:, None] & other_valid[None, :], sim, -3.0)
        row_best = jnp.max(masked.reshape(seq_len, count, seq_len), axis=2)
        prec = jnp.sum(my_weights_f[:, None] * row_best, axis=0) / my_total
        col_best = jnp.max(masked, axis=0).reshape(count, seq_len)
        other_f = some_weights.astype(jnp.float32)
        rec = jnp.sum(other_f * col_best, axis=1) / jnp.sum(other_f, axis=1)
        return (prec, rec)

    def one_block(pair):
        return block_scores(pair[0], pair[1])

    piece_units = lax.all_gather(units, ("samp", "tok"), axis=0, tiled=True)
    piece_weights = lax.all_gather(my_weights, ("samp", "tok"), axis=0, tiled=True)
    count = piece_units.shape[0] // seq_len
    group = 4
    block_units = piece_units.reshape(count // group, group, seq_len, width)
    block_weights = piece_weights.reshape(count // group, group, seq_len)
    found_prec, found_rec = lax.map(one_block, (block_units, block_weights))
    precision = found_prec.reshape(count)
    recall = found_rec.reshape(count)
    f_score = 2.0 * precision * recall / jnp.maximum(precision + recall, 0.25)
    own_score = lax.dynamic_index_in_dim(f_score, my_index, 0, keepdims=False)
    utility = (jnp.sum(f_score) - own_score) / (group_size - 1)
    return (
        embedded.reshape(1, seq_len, width),
        precision.reshape(1, group_size),
        recall.reshape(1, group_size),
        f_score.reshape(1, group_size),
        utility.reshape(1),
    )


def solution(mesh):
    placed = (
        P(("doc", "samp", "tok"), None, None),
        P(("doc", "samp", "tok"), None, None),
        P(None, ("samp", "tok")),
        P(),
        P(),
        P(),
        P(("doc", "samp", "tok"), None),
        P(("doc", "samp", "tok")),
        P(),
    )
    return jax.shard_map(
        local,
        mesh=mesh,
        in_specs=placed,
        out_specs=(
            P(("doc", "samp", "tok"), None, None),
            P(("doc", "samp", "tok"), None),
            P(("doc", "samp", "tok"), None),
            P(("doc", "samp", "tok"), None),
            P(("doc", "samp", "tok")),
        ),
        check_vma=False,
    )
```

profile of v0, /device:TPU:1, one launch (start us, length us, event | category | flops | bytes accessed | tf_op | source)
XLA Modules:
  0.0 203.8 jit_solution(18218272465197842143)
XLA Ops:
  7.2 0.7 all-gather.4.cloned.1.call-update
  8.0 75.5 %all-gather.4.cloned.1.call-done = bf16[1024,1024]{0,1:T(8,128)(2,1)} async-done(((bf16[1024,32]{0,1:T(8,128)(2,1)}), bf16[1024,1024]{0,1:T(8,128)(2,1)}) %all-gather.4.cloned.1.call-update) | async-done | bytes 2097168 | tf_op jit(solution)/shard_map/all_gather | solution.py:17
  83.5 2.5 %fusion.12 = (f32[128]{0:T(128)S(1)}, f32[128,1024]{1,0:T(8,128)S(1)}) fusion(f32[1024]{0:T(1024)} %param.14, bf16[1024,1024]{0,1:T(8,128)(2,1)} %all-gather.4.cloned.1.call-done, bf16[1,128,1024]{2,1,0:T(8,128)(2,1)S(1)} %copy-done, bf16[1,128,1024]{2,1,0:T(8,128)(2,1)} %param.12), kind=kOutput, calls=%fused_computation.38 | convolution fusion | flops 268959616 | bytes 3150336 | tf_op jit(solution)/shard_map/dot_general | solution.py:15
  86.0 0.2 multiply_reduce_fusion.1
  86.2 0.3 fusion.6
  86.5 0.8 fusion.7
  88.1 1.3 gather_fusion
  89.4 32.9 %all-gather = bf16[32,1,128]{2,1,0:T(2,128)(2,1)S(1)} all-gather(bf16[1,1,128]{2,1,0:T(2,128)(2,1)S(1)} %get-tuple-element.98), channel_id=1, replica_groups=mesh['doc'=16,'samp'=8,'tok'=4] {'samp','tok'}, dimensions={0}, use_global_device_ids=true | all-gather | bytes 8448 | tf_op jit(solution)/shard_map/all_gather | solution.py:53
  122.3 0.6 convert_reduce_fusion.1
  122.9 39.6 %all-gather.6.cloned.1.call-done = bf16[4096,1024]{1,0:T(8,128)(2,1)} async-done(((bf16[128,1024]{1,0:T(8,128)(2,1)}), bf16[4096,1024]{1,0:T(8,128)(2,1)}) %all-gather.6.cloned.1.call-update) | async-done | bytes 8388624 | tf_op jit(solution)/shard_map/all_gather | solution.py:52
  162.5 30.0 %while.13 = (s32[]{:T(128)}, f32[8,4]{1,0:T(8,128)S(1)}, f32[8,4]{1,0:T(8,128)S(1)}, f32[128]{0:T(128)S(1)}, bf16[8,4,128]{2,1,0:T(4,128)(2,1)S(1)}, /*index=5*/...) while((s32[]{:T(128)}, f32[8,4]{1,0:T(8,128)S(1)}, ...), condition=%wide.region_10.11_spmd.clone, body=%wide.region_4.10_spmd.clone.sunk | while | flops 134483072 | bytes 4994165 | solution.py:58
  162.5 1.3 constant_dynamic-slice_fusion.3
  163.9 0.7 iota_compare_fusion.2
  164.5 0.5 bitcast_reduce_fusion.2
  165.5 0.7 divide_bitcast_fusion.4
  166.3 1.3 constant_dynamic-slice_fusion.3
  167.6 0.7 iota_compare_fusion.2
  168.3 0.5 bitcast_reduce_fusion.2
  168.7 0.1 reduce_max.24
  169.3 0.7 divide_bitcast_fusion.4
  170.0 1.3 constant_dynamic-slice_fusion.3
  171.4 0.7 iota_compare_fusion.2
  172.0 0.5 bitcast_reduce_fusion.2
  172.5 0.1 reduce_max.24
  173.0 0.7 divide_bitcast_fusion.4
  173.8 1.3 constant_dynamic-slice_fusion.3
  175.1 0.7 iota_compare_fusion.2
  175.8 0.5 bitcast_reduce_fusion.2
  176.8 0.7 divide_bitcast_fusion.4
  177.5 1.3 constant_dynamic-slice_fusion.3
  178.9 0.7 iota_compare_fusion.2
  179.5 0.5 bitcast_reduce_fusion.2
  180.5 0.7 divide_bitcast_fusion.4
  181.3 1.3 constant_dynamic-slice_fusion.3
  182.6 0.7 iota_compare_fusion.2
  183.3 0.5 bitcast_reduce_fusion.2
  184.3 0.7 divide_bitcast_fusion.4
  185.0 1.3 constant_dynamic-slice_fusion.3
  186.4 0.7 iota_compare_fusion.2
  187.0 0.5 bitcast_reduce_fusion.2
  188.1 0.7 divide_bitcast_fusion.4
  188.8 1.3 constant_dynamic-slice_fusion.3
  190.1 0.7 iota_compare_fusion.2
  190.8 0.5 bitcast_reduce_fusion.2
  191.8 0.7 divide_bitcast_fusion.4
  192.7 0.6 divide_reduce_fusion
  193.5 0.6 dynamic_slice.12
  195.3 0.5 maximum_divide_fusion.1
  (111 shorter events, 5.0 us)
Async XLA Ops:
  7.2 76.3 %copy-start = (bf16[1,128,1024]{2,1,0:T(8,128)(2,1)S(1)}, bf16[1,128,1024]{2,1,0:T(8,128)(2,1)}, u32[]{:S(2)}) copy-start(bf16[1,128,1024]{2,1,0:T(8,128)(2,1)} %param.11) | copy-start | bytes 786436
  7.2 79.0 %copy-start.5 = (f32[1024]{0:T(1024)S(1)}, f32[1024]{0:T(1024)}, u32[]{:S(2)}) copy-start(f32[1024]{0:T(1024)} %param.15) | copy-start | bytes 12292
  7.2 79.0 %copy-start.4 = (f32[1024]{0:T(1024)S(1)}, f32[1024]{0:T(1024)}, u32[]{:S(2)}) copy-start(f32[1024]{0:T(1024)} %param.16) | copy-start | bytes 12292
  7.2 76.3 %all-gather.4.cloned.1.call-start = ((), (), s32[]{:S(2)}) async-start(), calls=%async_computation | async-start | bytes 2162688 | tf_op jit(solution)/shard_map/all_gather | solution.py:17
  7.9 80.1 %copy-start.8 = (s32[1,128]{1,0:T(1,128)S(1)}, s32[1,128]{1,0:T(1,128)}, u32[]{:S(2)}) copy-start(s32[1,128]{1,0:T(1,128)} %param.17) | copy-start | bytes 1540
  7.9 80.1 %copy-start.2 = (bf16[50265]{0:T(1024)(128)(2,1)S(1)}, bf16[50265]{0:T(1024)(128)(2,1)}, u32[]{:S(2)}) copy-start(bf16[50265]{0:T(1024)(128)(2,1)} %param.19) | copy-start | bytes 301594
  8.0 154.5 %all-gather.6.cloned.1.call-start = ((), (), s32[]{:S(2)}) async-start(), calls=%async_computation.1 | async-start | bytes 8650752 | tf_op jit(solution)/shard_map/all_gather | solution.py:52
  86.5 76.0 %copy-start.3 = (bf16[128,1024]{1,0:T(8,128)(2,1)}, bf16[128,1024]{1,0:T(8,128)(2,1)S(1)}, u32[]{:S(2)}) copy-start(bf16[128,1024]{1,0:T(8,128)(2,1)S(1)} %get-tuple-element.95) | copy-start | bytes 786436
  162.5 2.0 copy-start.1
  166.2 2.0 copy-start.1
  170.0 2.0 copy-start.1
  173.7 2.0 copy-start.1
  177.5 2.0 copy-start.1
  181.3 2.0 copy-start.1
  185.0 2.0 copy-start.1
  188.8 2.0 copy-start.1
  193.4 2.5 %copy-start.6 = (f32[1,32]{1,0:T(1,128)}, f32[1,32]{1,0:T(1,128)S(1)}, u32[]{:S(2)}) copy-start(f32[1,32]{1,0:T(1,128)S(1)} %reshape_reshape.6) | copy-start | bytes 388
  193.4 2.4 %copy-start.7 = (f32[1,32]{1,0:T(1,128)}, f32[1,32]{1,0:T(1,128)S(1)}, u32[]{:S(2)}) copy-start(f32[1,32]{1,0:T(1,128)S(1)} %reshape_reshape.7) | copy-start | bytes 388
Sparse Core Ops, SparseCore 0:
  10.2 73.2 all-gather.3
  87.5 74.9 all-gather.5
where the time goes:
time: 204 us
  waiting for transfers between devices  116 us (57%)
  blocking collectives  32.9 us (16%)
  other arithmetic  17.7 us (9%)
  between operations  17.3 us (8%)
  local copies, waits for them, and re-layouts  13.5 us (7%)
  matrix products  6.16 us (3%)
    all_gather x1, waiting for transfers between devices, local(): lax.all_gather(out_weight, ('samp', 'tok'), axis=1, tiled=True)  75.5 us
    all_gather x1, waiting for transfers between devices, local(): piece_units = lax.all_gather(units, ('samp', 'tok'), axis=0, tiled=True)  39.6 us
    all_gather x1, blocking collectives, local(): lax.all_gather(my_weights, ('samp', 'tok'), axis=0, tiled=True)  32.9 us
    dynamic_slice x8, local copies, waits for them, and re-layouts, local(): found_prec, found_rec = lax.map(one_block, (block_units, block_weights))  10.7 us
    lt x8, other arithmetic, local(): my_valid = positions < lengths[0]  5.22 us
    div x8, other arithmetic, block_scores(): prec = jnp.sum(my_weights_f[:, None] * row_best, axis=0) / my_total  5.2 us
  transfers between devices with their start and end apart: 2, of which 2 were waited for; matrix products, arithmetic and copies ran while one was open for 1% of the time, Pallas kernels for 0%

commit v1 on v0

v1 whole, which is shorter than its diff:
```python
import jax
import jax.numpy as jnp
from jax import lax
from jax.experimental import pallas as pl
from jax.experimental.pallas import tpu as pltpu
from jax.sharding import PartitionSpec as P

MESH = pl.DeviceIdType.MESH
F32 = jnp.float32
BF16 = jnp.bfloat16

SEQ = 128
WIDTH = 1024
RING = 8
SLICE = 32
SLOTS = 4
PIECE = 16
PIECES = 2 * SLICE // PIECE
CHUNKS = 4
ROWS = SEQ // CHUNKS
NT = (((1,), (1,)), ((), ()))

OWN, M1, M2, P1, C1, P2, C2 = range(7)
PLACES = {OWN: (0, 0), M1: (-1, 0), M2: (-2, 0), P1: (1, 0), C1: (1, 1), P2: (2, 0), C2: (2, 1)}
USED = [(OWN, 1), (M1, 0), (M1, 1), (M2, 0), (M2, 1), (P1, 0), (P1, 1), (C1, 0), (P2, 0), (C2, 0)]


def kernel(
    context_hbm, hidden_hbm, weight_hbm, bias_hbm, gain_hbm, shift_hbm, ids_hbm, length_hbm, table_hbm,
    embedded_out, scores_out,
    ctx, hid, wt, part, mixed, params, ids_ref, length_ref, flat, table, units, first_unit, tokw, result, arrived,
    load_sem, first_sem, chain_send, z_send, ctx_send, part_send, tokw_send, unit_send, result_send,
    slice_sem, z_sem, ctx_sem, part_sem, tokw_sem, unit_sem, result_sem,
):
    doc = lax.axis_index("doc")
    y = lax.axis_index("samp")
    tok = lax.axis_index("tok")
    z, c = tok // 2, tok % 2

    def device(dy, flip_z, flip_c):
        yy = (y + dy + RING) % RING
        zz = 1 - z if flip_z else z
        cc = 1 - c if flip_c else c
        return (doc, yy, zz * 2 + cc)

    def number(blk, s):
        dy = jnp.where(blk <= M2, -blk, (blk - 1) // 2)
        flip = jnp.where((blk == C1) | (blk == C2), 1, 0)
        return (y + dy + RING) % RING * 4 + (z + flip) % 2 * 2 + (c + s) % 2

    up, down, inner, mate = device(1, 0, 0), device(-1, 0, 0), device(0, 1, 0), device(0, 0, 1)
    ahead = device(1 - 2 * c, 0, 0)

    def rows_of(zz, piece):
        return pl.ds(pl.multiple_of(zz * 2 * SLICE + piece * PIECE, PIECE), PIECE)

    def own_piece(h):
        return weight_hbm.at[pl.ds(h * PIECE, PIECE)], wt.at[0, rows_of(z, c * 2 + h)]

    @pl.when(c == 0)
    def _():
        for h in (0, 1):
            pltpu.make_async_copy(*own_piece(h), slice_sem.at[0, h]).start()

    loads = [
        pltpu.make_async_copy(context_hbm.at[0], ctx.at[0], load_sem.at[0]),
        pltpu.make_async_copy(table_hbm, flat, load_sem.at[1]),
        pltpu.make_async_copy(ids_hbm, ids_ref, load_sem.at[2]),
        pltpu.make_async_copy(length_hbm, length_ref, load_sem.at[3]),
        pltpu.make_async_copy(hidden_hbm.at[0], hid, load_sem.at[4]),
        pltpu.make_async_copy(bias_hbm, params.at[0], load_sem.at[5]),
        pltpu.make_async_copy(gain_hbm, params.at[1], load_sem.at[6]),
        pltpu.make_async_copy(shift_hbm, params.at[2], load_sem.at[7]),
    ]
    for load in loads:
        load.start()

    partners = [inner, mate]
    partners += [device(dy, 0, fc) for dy in (1, -1, 2, -2) for fc in (0, 1)]
    partners += [device(dy, 1, 0) for dy in (1, -1, 2, -2)]
    barrier = pltpu.get_barrier_semaphore()
    for partner in partners:
        pl.semaphore_signal(barrier, inc=1, device_id=partner, device_id_type=MESH)

    def remote(src, dst, send_sem, recv_sem, target):
        return pltpu.make_async_remote_copy(
            src_ref=src, dst_ref=dst, send_sem=send_sem, recv_sem=recv_sem,
            device_id=target, device_id_type=MESH,
        )

    def landed(dst, recv_sem):
        remote(dst, dst, ctx_send, recv_sem, mate).wait_recv()

    def sent(src, send_sem):
        remote(src, src, send_sem, ctx_sem, mate).wait_send()

    result[...] = jnp.zeros_like(result)
    pl.semaphore_wait(barrier, len(partners))

    below = (doc, (y + RING - 1) % RING, z * 2 + 1)

    for h in (0, 1):
        @pl.when(c == 0)
        def _(h=h):
            remote(*own_piece(h), first_sem.at[1, h], slice_sem.at[0, h], below).start()

        @pl.when(c == 1)
        def _(h=h):
            remote(*own_piece(h), first_sem.at[1, h], slice_sem.at[0, 2 + h], below).start()
            remote(*own_piece(h), first_sem.at[0, h], slice_sem.at[0, 2 + h], mate).start()

    loads[0].wait()
    remote(ctx.at[0], ctx.at[1], ctx_send, ctx_sem, mate).start()

    def columns_at(k, core):
        yy = (y + RING + jnp.where(core == 0, -k, k + 1)) % RING
        return pl.ds(pl.multiple_of(yy * SEQ, SEQ), SEQ)

    lane = lax.broadcasted_iota(jnp.int32, (1, SEQ), 1)

    def token_weights():
        for load in loads[1:4]:
            load.wait()
        vocab = flat.shape[0]
        full = vocab // WIDTH
        table[pl.ds(full * 8, 16)] = jnp.zeros((16, SEQ), BF16)

        @pl.loop(0, full)
        def _(k):
            table[pl.ds(pl.multiple_of(k * 8, 8), 8)] = flat[
                pl.ds(pl.multiple_of(k * WIDTH, WIDTH), WIDTH)
            ].reshape(8, SEQ)

        for k in range(full * 8, -(-vocab // SEQ)):
            count = min(SEQ, vocab - k * SEQ)
            table[k:k + 1, :count] = flat[pl.ds(k * SEQ, count)].reshape(1, count)
        ids = ids_ref[...]
        chosen = lax.broadcasted_iota(jnp.int32, (SEQ, SEQ), 0) == (ids & (SEQ - 1))
        columns = jnp.dot(
            table[...], jnp.where(chosen, 1.0, 0.0).astype(BF16), preferred_element_type=F32
        )
        row_hit = lax.broadcasted_iota(jnp.int32, columns.shape, 0) == (ids >> 7)
        found = jnp.sum(jnp.where(row_hit, columns, 0.0), axis=0, keepdims=True)
        own = jnp.where(lane < length_ref[0], found, 0.0)
        own = own / jnp.sum(own, axis=1, keepdims=True)
        tokw[OWN, 0] = jnp.broadcast_to(own, (8, SEQ))
        for k, (blk, s) in enumerate(USED):
            dy, flip_z = PLACES[blk]
            remote(
                tokw.at[OWN, 0], tokw.at[blk, s], tokw_send.at[k], tokw_sem.at[blk, s], device(-dy, flip_z, s)
            ).start()

    @pl.loop(0, SLOTS + 1)
    def _(k):
        @pl.when(k < SLOTS)
        def _():
            for s in range(PIECES):
                rows = rows_of(z, s)
                landed(wt.at[k, rows], slice_sem.at[k, s])

                @pl.when(k + 1 < SLOTS)
                def _(rows=rows, s=s):
                    remote(
                        wt.at[k, rows], wt.at[k + 1, rows], chain_send.at[k, s], slice_sem.at[k + 1, s], ahead
                    ).start()

                remote(wt.at[k, rows], wt.at[k, rows], z_send.at[k, s], z_sem.at[k, s], inner).start()

        @pl.when(k == 2)
        def _():
            landed(ctx.at[1], ctx_sem)

        @pl.when(k == 3)
        def _():
            token_weights()

        @pl.when((k == 2) | (k == 4))
        def _():
            for n in (0, 1):
                for s in range(PIECES):
                    landed(wt.at[k - 2 + n, rows_of(1 - z, s)], z_sem.at[k - 2 + n, s])
            both = lax.dot_general(
                ctx[...].reshape(2 * SEQ, WIDTH), wt[pl.ds(k - 2, 2)].reshape(2 * SEQ, WIDTH), NT,
                preferred_element_type=F32,
            )
            for n in (0, 1):
                at = columns_at(k - 2 + n, c)
                side = slice(n * SEQ, (n + 1) * SEQ)
                part[k - 2 + n] = both[SEQ:, side]
                remote(
                    part.at[k - 2 + n], mixed.at[:, at], part_send.at[k - 2 + n], part_sem.at[k - 2 + n], mate
                ).start()
                mixed[:, at] = both[:SEQ, side]

    for load in loads[4:]:
        load.wait()
    for k in range(SLOTS):
        landed(mixed.at[:, columns_at(k, 1 - c)], part_sem.at[k])

    def slot(blk, s, q):
        return units.at[blk, s, pl.ds(pl.multiple_of(q * ROWS, ROWS), ROWS)]

    moves = []

    def pass_on(src, dst, q, target):
        if (src, dst) not in moves:
            moves.append((src, dst))
        remote(
            slot(*src, q), slot(*dst, q), unit_send.at[moves.index((src, dst)), q],
            unit_sem.at[dst[0], dst[1], q], target,
        ).start()

    @pl.loop(0, CHUNKS)
    def _(q):
        rows = pl.ds(pl.multiple_of(q * ROWS, ROWS), ROWS)
        x = hid[rows, :].astype(F32) + mixed[rows, :] + params[0]
        centre = x - jnp.mean(x, axis=-1, keepdims=True)
        spread = jnp.mean(centre * centre, axis=-1, keepdims=True)
        embedded = (centre * lax.rsqrt(spread + 1e-07) * params[1] + params[2]).astype(BF16)
        embedded_out[0, rows, :] = embedded
        values = embedded.astype(F32)
        unit = values * lax.rsqrt(jnp.sum(values * values, axis=-1, keepdims=True) + 1e-06)

        @pl.when(q == 0)
        def _():
            first_unit[...] = unit[:1]

        real = lax.broadcasted_iota(jnp.int32, (ROWS, 1), 0) + q * ROWS < length_ref[0]
        units[OWN, 0, rows] = jnp.where(real, unit, first_unit[...]).astype(BF16)
        pass_on((OWN, 0), (M1, 0), q, up)
        pass_on((OWN, 0), (P1, 0), q, down)
        pass_on((OWN, 0), (OWN, 1), q, mate)

    def all_landed(blk, s):
        for q in range(CHUNKS):
            landed(slot(blk, s, q), unit_sem.at[blk, s, q])

    eye = lax.broadcasted_iota(jnp.int32, (SEQ, SEQ), 0) == lax.broadcasted_iota(jnp.int32, (SEQ, SEQ), 1)
    line = lax.broadcasted_iota(jnp.int32, (8, SEQ), 0)

    def two_lines(first, second):
        return jnp.where(line == 0, first, jnp.where(line == 1, second, 0.0))

    def score(sim, a, b, to_a=True):
        best_a = jnp.sum(jnp.where(eye, jnp.max(sim, axis=1, keepdims=True), 0.0), axis=0, keepdims=True)
        best_b = jnp.max(sim, axis=0, keepdims=True)
        p = jnp.sum(tokw[a[0], a[1], 0:1] * best_a, axis=1, keepdims=True)
        r = jnp.sum(tokw[b[0], b[1], 0:1] * best_b, axis=1, keepdims=True)
        lane_b = number(*b) if to_a is True else jnp.where(to_a, number(*b), -1)
        lane_a = number(*a)
        result[a[0], a[1]] = result[a[0], a[1]] + jnp.where(lane == lane_b, two_lines(p, r), 0.0)
        result[b[0], b[1]] = result[b[0], b[1]] + jnp.where(lane == lane_a, two_lines(r, p), 0.0)

    def single(blk, s, other):
        score(
            lax.dot_general(units[blk, s], units[other, 0], NT, preferred_element_type=F32), (blk, s), (other, 0)
        )

    def double(blk, s, other, keep_self=True):
        sims = lax.dot_general(
            units[blk, s], units[pl.ds(other, 2), 0].reshape(2 * SEQ, WIDTH), NT, preferred_element_type=F32
        )
        score(sims[:, :SEQ], (blk, s), (other, 0), keep_self)
        score(sims[:, SEQ:], (blk, s), (other + 1, 0))

    @pl.loop(0, 2 * CHUNKS)
    def _(t):
        @pl.when(t < CHUNKS)
        def _():
            q = t
            landed(slot(M1, 0, q), unit_sem.at[M1, 0, q])
            pass_on((M1, 0), (M2, 0), q, up)
            landed(slot(P1, 0, q), unit_sem.at[P1, 0, q])
            pass_on((P1, 0), (P2, 0), q, down)
            pass_on((P1, 0), (C1, 0), q, inner)
            pass_on((M1, 0), (M1, 1), q, mate)
            pass_on((P1, 0), (P1, 1), q, mate)

        @pl.when(t >= CHUNKS)
        def _():
            q = t - CHUNKS
            landed(slot(P2, 0, q), unit_sem.at[P2, 0, q])
            pass_on((P2, 0), (C2, 0), q, inner)
            landed(slot(M2, 0, q), unit_sem.at[M2, 0, q])
            pass_on((M2, 0), (M2, 1), q, mate)

        @pl.when(t == 2)
        def _():
            for blk, s in USED:
                landed(tokw.at[blk, s], tokw_sem.at[blk, s])

        for when, blk, s in ((4, OWN, 1), (5, C1, 0), (6, M1, 1)):
            @pl.when(t == when)
            def _(blk=blk, s=s):
                all_landed(blk, s)

        @pl.when(t >= 3)
        def _():
            left = jnp.where(t <= 4, OWN, jnp.where(t <= 6, M1, M2))
            sample = jnp.where((t == 4) | (t == 6), 1, 0)
            double(left, sample, jnp.where(t <= 4, OWN, P1), t >= 5)

    all_landed(P1, 1)

    @pl.loop(0, 3)
    def _(t):
        single(jnp.where(t < 2, OWN, P1), jnp.where(t < 2, t, z), C1)

    all_landed(M2, 1)
    double(M2, 1, P1)

    @pl.loop(0, 2)
    def _(t):
        @pl.when(t == 1)
        def _():
            all_landed(C2, 0)

        single(M2, jnp.where(t == 0, y // 4, z), P2 + t)

    for k, (blk, s) in enumerate(USED):
        dy, flip_z = PLACES[blk]
        remote(
            result.at[blk, s], arrived.at[k], result_send.at[k], result_sem.at[k], device(dy, flip_z, s)
        ).start()
    for k in range(len(USED)):
        landed(arrived.at[k], result_sem.at[k])
    everything = result[OWN, 0]
    for k in range(len(USED)):
        everything = everything + arrived[k]
    precision = everything[0:1]
    recall = everything[1:2]
    f_score = 2.0 * precision * recall / jnp.maximum(precision + recall, 0.25)
    others = jnp.where((lane < 32) & (lane != number(OWN, 0)), f_score, 0.0)
    utility = jnp.sum(others, axis=1, keepdims=True) / 31.0
    scores_out[...] = jnp.where(line < 2, everything, jnp.where(line == 2, f_score, utility))

    @pl.loop(0, CHUNKS)
    def _(q):
        for m, (src, _) in enumerate(moves):
            sent(slot(*src, q), unit_send.at[m, q])

    for k in range(SLOTS):
        for s in range(PIECES):
            piece = wt.at[k, rows_of(z, s)]
            if k + 1 < SLOTS:
                sent(piece, chain_send.at[k, s])
            sent(piece, z_send.at[k, s])
        sent(part.at[k], part_send.at[k])
    sent(ctx.at[0], ctx_send)
    for k, (blk, s) in enumerate(USED):
        sent(tokw.at[OWN, 0], tokw_send.at[k])
        sent(result.at[blk, s], result_send.at[k])
    for h in (0, 1):
        sent(own_piece(h)[0], first_sem.at[1, h])

    @pl.when(c == 1)
    def _():
        for h in (0, 1):
            sent(own_piece(h)[0], first_sem.at[0, h])


def hand_out(embedded_ref, scores_ref, embedded_hbm, precision_ref, recall_ref, f_ref, utility_ref, sem):
    copy = pltpu.make_async_copy(embedded_ref, embedded_hbm, sem)
    copy.start()
    precision_ref[...] = scores_ref[0:1, :32]
    recall_ref[...] = scores_ref[1:2, :32]
    f_ref[...] = scores_ref[2:3, :32]
    utility_ref[...] = scores_ref[3:4, :1]
    copy.wait()


def local(
    context, hidden, out_weight, out_bias, norm_gain, norm_bias, token_ids, lengths, idf_table
):
    vocab = idf_table.shape[0]
    table_rows = vocab // WIDTH * 8 + 16
    vmem = pl.BlockSpec(memory_space=pltpu.VMEM)
    hbm = pl.BlockSpec(memory_space=pl.ANY)
    dma = pltpu.SemaphoreType.DMA
    count = len(USED)
    embedded, scores = pl.pallas_call(
        kernel,
        out_shape=(
            jax.ShapeDtypeStruct((1, SEQ, WIDTH), BF16),
            jax.ShapeDtypeStruct((8, SEQ), F32),
        ),
        in_specs=[hbm] * 9,
        out_specs=(vmem, vmem),
        scratch_shapes=[
            pltpu.VMEM((2, SEQ, WIDTH), BF16),
            pltpu.VMEM((SEQ, WIDTH), BF16),
            pltpu.VMEM((SLOTS, SEQ, WIDTH), BF16),
            pltpu.VMEM((SLOTS, SEQ, SEQ), F32),
            pltpu.VMEM((SEQ, WIDTH), F32),
            pltpu.VMEM((3, 1, WIDTH), F32),
            pltpu.VMEM((1, SEQ), jnp.int32),
            pltpu.SMEM((1,), jnp.int32),
            pltpu.VMEM((vocab,), BF16),
            pltpu.VMEM((table_rows, SEQ), BF16),
            pltpu.VMEM((7, 2, SEQ, WIDTH), BF16),
            pltpu.VMEM((1, WIDTH), F32),
            pltpu.VMEM((7, 2, 8, SEQ), F32),
            pltpu.VMEM((7, 2, 8, SEQ), F32),
            pltpu.VMEM((count, 8, SEQ), F32),
            dma((8,)),
            dma((2, 2)),
            dma((SLOTS - 1, PIECES)),
            dma((SLOTS, PIECES)),
            dma,
            dma((SLOTS,)),
            dma((count,)),
            dma((10, CHUNKS)),
            dma((count,)),
            dma((SLOTS, PIECES)),
            dma((SLOTS, PIECES)),
            dma,
            dma((SLOTS,)),
            dma((7, 2)),
            dma((7, 2, CHUNKS)),
            dma((count,)),
        ],
        compiler_params=pltpu.CompilerParams(
            collective_id=0, has_side_effects=True, vmem_limit_bytes=60 * 1024 * 1024
        ),
        cost_estimate=pl.CostEstimate(flops=1 << 30, bytes_accessed=1 << 20, transcendentals=0),
    )(
        context, hidden, out_weight.T, out_bias.reshape(1, WIDTH), norm_gain.reshape(1, WIDTH),
        norm_bias.reshape(1, WIDTH), token_ids, lengths, idf_table,
    )
    embedded, precision, recall, f_score, utility = pl.pallas_call(
        hand_out,
        out_shape=(
            jax.ShapeDtypeStruct((1, SEQ, WIDTH), BF16),
            jax.ShapeDtypeStruct((1, 32), F32),
            jax.ShapeDtypeStruct((1, 32), F32),
            jax.ShapeDtypeStruct((1, 32), F32),
            jax.ShapeDtypeStruct((1, 1), F32),
        ),
        in_specs=[vmem, vmem],
        out_specs=(pl.BlockSpec(memory_space=pl.ANY), vmem, vmem, vmem, vmem),
        scratch_shapes=[dma],
    )(embedded, scores)
    return embedded, precision, recall, f_score, utility.reshape(1)


def solution(mesh):
    placed = (
        P(("doc", "samp", "tok"), None, None),
        P(("doc", "samp", "tok"), None, None),
        P(None, ("samp", "tok")),
        P(),
        P(),
        P(),
        P(("doc", "samp", "tok"), None),
        P(("doc", "samp", "tok")),
        P(),
    )
    return jax.shard_map(
        local,
        mesh=mesh,
        in_specs=placed,
        out_specs=(
            P(("doc", "samp", "tok"), None, None),
            P(("doc", "samp", "tok"), None),
            P(("doc", "samp", "tok"), None),
            P(("doc", "samp", "tok"), None),
            P(("doc", "samp", "tok")),
        ),
        check_vma=False,
    )
```

time: 204 us -> 53.1 us (0.26)
  waiting for transfers between devices: 116 us -> 0 us
  Pallas kernels: 0 us -> 51.6 us
  blocking collectives: 32.9 us -> 0 us
  other arithmetic: 17.7 us -> 0 us
  between operations: 17.3 us -> 1.29 us
  local copies, waits for them, and re-layouts: 13.5 us -> 0 us
  matrix products: 6.16 us -> 0 us
    all_gather x2 -> x0, waiting for transfers between devices: 115 us -> none  [the longest x1 75.5 us: local(): lax.all_gather(out_weight, ('samp', 'tok'), axis=1, tiled=True)]
    pallas_call x0 -> x2, Pallas kernels: none -> 51.6 us  [the longest x1 49.4 us: local(): pl.pallas_call(kernel, out_shape=(jax.ShapeDtypeStruct((1, SEQ, WIDTH), B...]
    all_gather x1 -> x0, blocking collectives: 32.9 us -> none  [local(): lax.all_gather(my_weights, ('samp', 'tok'), axis=0, tiled=True)]
    dynamic_slice x9 -> x0, local copies, waits for them, and re-layouts: 11.3 us -> none  [the longest x8 10.7 us: local(): found_prec, found_rec = lax.map(one_block, (block_units, block_weights))]
    dot_general x9 -> x0, matrix products: 6.16 us -> none  [the longest x8 3.64 us: block_scores(): lax.dot_general(units, flat_units, (((1,), (1,)), ((), ())), preferred_el...]
    div x19 -> x0, other arithmetic: 5.8 us -> none  [the longest x8 5.2 us: block_scores(): prec = jnp.sum(my_weights_f[:, None] * row_best, axis=0) / my_total]
    lt x8 -> x0, other arithmetic: 5.22 us -> none  [local(): my_valid = positions < lengths[0]]
    reduce_sum x28 -> x0, other arithmetic: 4.5 us -> none  [the longest x16 1.91 us: block_scores(): rec = jnp.sum(other_f * col_best, axis=1) / jnp.sum(other_f, axis=1)]
  transfers between devices with their start and end apart: 2 -> 0, of which waited for: 2 -> 0; matrix products, arithmetic and copies ran while one was open for 1% -> 0% of each run, Pallas kernels for 0% -> 0%
where the time goes in v1:
time: 53.1 us; the launch traced here: 52.9 us
  Pallas kernels  51.6 us (97%)
  between operations  1.29 us (2%)
    pallas_call x1, Pallas kernels, local(): pl.pallas_call(kernel, out_shape=(jax.ShapeDtypeStruct((1, SEQ, WIDTH), B...  49.4 us
    pallas_call x1, Pallas kernels, local(): pl.pallas_call(hand_out, out_shape=(jax.ShapeDtypeStruct((1, SEQ, WIDTH),...  2.19 us

profile of v1, /device:TPU:1, one launch (start us, length us, event | category | flops | bytes accessed | tf_op | source)
XLA Modules:
  0.0 52.9 jit_solution(12176524113201802546)
XLA Ops:
  1.3 49.4 %shard_map.128 = (bf16[1,128,1024]{2,1,0:T(8,128)(2,1)}, f32[8,128]{1,0:T(8,128)}) custom-call(bf16[1,128,1024]{2,1,0:T(8,128)(2,1)} %context_hbm.1, bf16[1,128,1024]{2,1,0:T(8,128)(2,1)} %hidden_hbm.1, bf16[32,1024]{1,0:T(8,128)(2,1)} %bitcast.5, f32[1,1024]{1,0:T(1,128)} %bitcast.6, f32[1,1024]{1,0:T(1,128)} %bitcast.7, f32[1,1024]{1,0:T(1,128)} %bitcast.8, ...), custom_call_target="tpu_custom_call" | custom-call | flops 1073741824 | bytes 1048576 | tf_op jit(solution)/shard_map/pallas_call | solution.py:381
  50.7 2.2 %shard_map.129 = (bf16[1,128,1024]{2,1,0:T(8,128)(2,1)}, f32[1,32]{1,0:T(1,128)}, f32[1,32]{1,0:T(1,128)}, f32[1,32]{1,0:T(1,128)}, f32[1,1]{1,0:T(1,128)}) custom-call(bf16[1,128,1024]{2,1,0:T(8,128)(2,1)} %get-tuple-element.12.embedded_ref, f32[8,128]{1,0:T(8,128)} %get-tuple-element.13.scores_ref), custom_call_target="tpu_custom_call" | custom-call | tf_op jit(solution)/shard_map/pallas_call | solution.py:430

commit v2 on v1

--- a/solution.py
+++ b/solution.py
@@ -29,7 +29,7 @@
     context_hbm, hidden_hbm, weight_hbm, bias_hbm, gain_hbm, shift_hbm, ids_hbm, length_hbm, table_hbm,
     embedded_out, scores_out,
     ctx, hid, wt, part, mixed, params, ids_ref, length_ref, flat, table, units, first_unit, tokw, result, arrived,
-    load_sem, first_sem, chain_send, z_send, ctx_send, part_send, tokw_send, unit_send, result_send,
+    load_sem, first_sem, chain_send, z_send, side_send, ctx_send, part_send, tokw_send, unit_send, result_send,
     slice_sem, z_sem, ctx_sem, part_sem, tokw_sem, unit_sem, result_sem,
 ):
     doc = lax.axis_index("doc")
@@ -164,33 +164,48 @@
                         wt.at[k, rows], wt.at[k + 1, rows], chain_send.at[k, s], slice_sem.at[k + 1, s], ahead
                     ).start()
 
-                remote(wt.at[k, rows], wt.at[k, rows], z_send.at[k, s], z_sem.at[k, s], inner).start()
-
-        @pl.when(k == 2)
+                @pl.when((k == 0) | (s < PIECES // 2))
+                def _(rows=rows, s=s):
+                    remote(wt.at[k, rows], wt.at[k, rows], z_send.at[k, s], z_sem.at[k, s], inner).start()
+
+        @pl.when(k >= 1)
+        def _():
+            for s in range(PIECES // 2, PIECES):
+                rows = rows_of(1 - z, s)
+                landed(wt.at[k - 1, rows], z_sem.at[k - 1, s])
+
+                @pl.when(k < SLOTS)
+                def _(rows=rows, s=s):
+                    remote(
+                        wt.at[k - 1, rows], wt.at[k, rows], side_send.at[k - 1, s - PIECES // 2], z_sem.at[k, s], ahead
+                    ).start()
+
+        @pl.when(k == 3)
         def _():
             landed(ctx.at[1], ctx_sem)
 
-        @pl.when(k == 3)
-        def _():
-            token_weights()
-
-        @pl.when((k == 2) | (k == 4))
-        def _():
+        @pl.when(k >= 3)
+        def _():
+            first = (k - 3) * 2
             for n in (0, 1):
-                for s in range(PIECES):
-                    landed(wt.at[k - 2 + n, rows_of(1 - z, s)], z_sem.at[k - 2 + n, s])
+                for s in range(PIECES // 2):
+                    landed(wt.at[first + n, rows_of(1 - z, s)], z_sem.at[first + n, s])
             both = lax.dot_general(
-                ctx[...].reshape(2 * SEQ, WIDTH), wt[pl.ds(k - 2, 2)].reshape(2 * SEQ, WIDTH), NT,
+                ctx[...].reshape(2 * SEQ, WIDTH), wt[pl.ds(first, 2)].reshape(2 * SEQ, WIDTH), NT,
                 preferred_element_type=F32,
             )
             for n in (0, 1):
-                at = columns_at(k - 2 + n, c)
+                at = columns_at(first + n, c)
                 side = slice(n * SEQ, (n + 1) * SEQ)
-                part[k - 2 + n] = both[SEQ:, side]
+                part[first + n] = both[SEQ:, side]
                 remote(
-                    part.at[k - 2 + n], mixed.at[:, at], part_send.at[k - 2 + n], part_sem.at[k - 2 + n], mate
+                    part.at[first + n], mixed.at[:, at], part_send.at[first + n], part_sem.at[first + n], mate
                 ).start()
                 mixed[:, at] = both[:SEQ, side]
+
+        @pl.when(k == 3)
+        def _():
+            token_weights()
 
     for load in loads[4:]:
         load.wait()
@@ -231,6 +246,26 @@
         pass_on((OWN, 0), (P1, 0), q, down)
         pass_on((OWN, 0), (OWN, 1), q, mate)
 
+    for k in range(SLOTS):
+        for s in range(PIECES):
+            if k + 1 < SLOTS:
+                sent(wt.at[k, rows_of(z, s)], chain_send.at[k, s])
+                if s >= PIECES // 2:
+                    sent(wt.at[k, rows_of(1 - z, s)], side_send.at[k, s - PIECES // 2])
+            if k == 0 or s < PIECES // 2:
+                sent(wt.at[k, rows_of(z, s)], z_send.at[k, s])
+        sent(part.at[k], part_send.at[k])
+    sent(ctx.at[0], ctx_send)
+    for k in range(len(USED)):
+        sent(tokw.at[OWN, 0], tokw_send.at[k])
+    for h in (0, 1):
+        sent(own_piece(h)[0], first_sem.at[1, h])
+
+    @pl.when(c == 1)
+    def _():
+        for h in (0, 1):
+            sent(own_piece(h)[0], first_sem.at[0, h])
+
     def all_landed(blk, s):
         for q in range(CHUNKS):
             landed(slot(blk, s, q), unit_sem.at[blk, s, q])
@@ -322,6 +357,13 @@
         remote(
             result.at[blk, s], arrived.at[k], result_send.at[k], result_sem.at[k], device(dy, flip_z, s)
         ).start()
+    @pl.loop(0, CHUNKS)
+    def _(q):
+        for m, (src, _) in enumerate(moves):
+            sent(slot(*src, q), unit_send.at[m, q])
+
+    for k, (blk, s) in enumerate(USED):
+        sent(result.at[blk, s], result_send.at[k])
     for k in range(len(USED)):
         landed(arrived.at[k], result_sem.at[k])
     everything = result[OWN, 0]
@@ -333,30 +375,6 @@
     others = jnp.where((lane < 32) & (lane != number(OWN, 0)), f_score, 0.0)
     utility = jnp.sum(others, axis=1, keepdims=True) / 31.0
     scores_out[...] = jnp.where(line < 2, everything, jnp.where(line == 2, f_score, utility))
-
-    @pl.loop(0, CHUNKS)
-    def _(q):
-        for m, (src, _) in enumerate(moves):
-            sent(slot(*src, q), unit_send.at[m, q])
-
-    for k in range(SLOTS):
-        for s in range(PIECES):
-            piece = wt.at[k, rows_of(z, s)]
-            if k + 1 < SLOTS:
-                sent(piece, chain_send.at[k, s])
-            sent(piece, z_send.at[k, s])
-        sent(part.at[k], part_send.at[k])
-    sent(ctx.at[0], ctx_send)
-    for k, (blk, s) in enumerate(USED):
-        sent(tokw.at[OWN, 0], tokw_send.at[k])
-        sent(result.at[blk, s], result_send.at[k])
-    for h in (0, 1):
-        sent(own_piece(h)[0], first_sem.at[1, h])
-
-    @pl.when(c == 1)
-    def _():
-        for h in (0, 1):
-            sent(own_piece(h)[0], first_sem.at[0, h])
 
 
 def hand_out(embedded_ref, scores_ref, embedded_hbm, precision_ref, recall_ref, f_ref, utility_ref, sem):
@@ -406,6 +424,7 @@
             dma((2, 2)),
             dma((SLOTS - 1, PIECES)),
             dma((SLOTS, PIECES)),
+            dma((SLOTS - 1, PIECES // 2)),
             dma,
             dma((SLOTS,)),
             dma((count,)),

time: 53.1 us -> 52.3 us (0.985)
  Pallas kernels: 51.6 us -> 50.8 us
    pallas_call x1, Pallas kernels: 49.4 us -> 48.6 us  [local(): pl.pallas_call(kernel, out_shape=(jax.ShapeDtypeStruct((1, SEQ, WIDTH), B...]
where the time goes in v2:
time: 52.3 us; the launch traced here: 52.1 us
  Pallas kernels  50.8 us (97%)
  between operations  1.29 us (2%)
    pallas_call x1, Pallas kernels, local(): pl.pallas_call(kernel, out_shape=(jax.ShapeDtypeStruct((1, SEQ, WIDTH), B...  48.6 us
    pallas_call x1, Pallas kernels, local(): pl.pallas_call(hand_out, out_shape=(jax.ShapeDtypeStruct((1, SEQ, WIDTH),...  2.19 us

profile of v2, /device:TPU:1, one launch (start us, length us, event | category | flops | bytes accessed | tf_op | source)
XLA Modules:
  0.0 52.1 jit_solution(1403086868455436036)
XLA Ops:
  1.3 48.6 %shard_map.128 = (bf16[1,128,1024]{2,1,0:T(8,128)(2,1)}, f32[8,128]{1,0:T(8,128)}) custom-call(bf16[1,128,1024]{2,1,0:T(8,128)(2,1)} %context_hbm.1, bf16[1,128,1024]{2,1,0:T(8,128)(2,1)} %hidden_hbm.1, bf16[32,1024]{1,0:T(8,128)(2,1)} %bitcast.5, f32[1,1024]{1,0:T(1,128)} %bitcast.6, f32[1,1024]{1,0:T(1,128)} %bitcast.7, f32[1,1024]{1,0:T(1,128)} %bitcast.8, ...), custom_call_target="tpu_custom_call" | custom-call | flops 1073741824 | bytes 1048576 | tf_op jit(solution)/shard_map/pallas_call | solution.py:399
  49.9 2.2 %shard_map.129 = (bf16[1,128,1024]{2,1,0:T(8,128)(2,1)}, f32[1,32]{1,0:T(1,128)}, f32[1,32]{1,0:T(1,128)}, f32[1,32]{1,0:T(1,128)}, f32[1,1]{1,0:T(1,128)}) custom-call(bf16[1,128,1024]{2,1,0:T(8,128)(2,1)} %get-tuple-element.12.embedded_ref, f32[8,128]{1,0:T(8,128)} %get-tuple-element.13.scores_ref), custom_call_target="tpu_custom_call" | custom-call | tf_op jit(solution)/shard_map/pallas_call | solution.py:449

commit v3 on v2

--- a/solution.py
+++ b/solution.py
@@ -22,14 +22,14 @@
 
 OWN, M1, M2, P1, C1, P2, C2 = range(7)
 PLACES = {OWN: (0, 0), M1: (-1, 0), M2: (-2, 0), P1: (1, 0), C1: (1, 1), P2: (2, 0), C2: (2, 1)}
-USED = [(OWN, 1), (M1, 0), (M1, 1), (M2, 0), (M2, 1), (P1, 0), (P1, 1), (C1, 0), (P2, 0), (C2, 0)]
+USED = [(OWN, 1), (M1, 0), (M1, 1), (M2, 0), (M2, 1), (P1, 0), (C1, 0), (P2, 0), (C2, 0)]
 
 
 def kernel(
     context_hbm, hidden_hbm, weight_hbm, bias_hbm, gain_hbm, shift_hbm, ids_hbm, length_hbm, table_hbm,
     embedded_out, scores_out,
-    ctx, hid, wt, part, mixed, params, ids_ref, length_ref, flat, table, units, first_unit, tokw, result, arrived,
-    load_sem, first_sem, chain_send, z_send, side_send, ctx_send, part_send, tokw_send, unit_send, result_send,
+    ctx, hid, wt, part, mixed, params, ids_ref, length_ref, flat, table, emb, units, first_unit, tokw, result, arrived,
+    load_sem, store_sem, first_sem, chain_send, z_send, side_send, ctx_send, part_send, tokw_send, unit_send, result_send,
     slice_sem, z_sem, ctx_sem, part_sem, tokw_sem, unit_sem, result_sem,
 ):
     doc = lax.axis_index("doc")
@@ -40,16 +40,24 @@
     def device(dy, flip_z, flip_c):
         yy = (y + dy + RING) % RING
         zz = 1 - z if flip_z else z
-        cc = 1 - c if flip_c else c
-        return (doc, yy, zz * 2 + cc)
+        return (doc, yy, zz * 2 + (c + flip_c) % 2)
+
+    def holder(blk, s):
+        dy, flip_z = PLACES[blk]
+        return device(-dy, flip_z, s + (1 - z if flip_z else 0))
+
+    def owner(blk, s):
+        dy, flip_z = PLACES[blk]
+        return device(dy, flip_z, s + (z if flip_z else 0))
 
     def number(blk, s):
         dy = jnp.where(blk <= M2, -blk, (blk - 1) // 2)
         flip = jnp.where((blk == C1) | (blk == C2), 1, 0)
-        return (y + dy + RING) % RING * 4 + (z + flip) % 2 * 2 + (c + s) % 2
+        return (y + dy + RING) % RING * 4 + (z + flip) % 2 * 2 + (c + s + flip * z) % 2
 
     up, down, inner, mate = device(1, 0, 0), device(-1, 0, 0), device(0, 1, 0), device(0, 0, 1)
     ahead = device(1 - 2 * c, 0, 0)
+    across = device(0, 1, 1 - z)
 
     def rows_of(zz, piece):
         return pl.ds(pl.multiple_of(zz * 2 * SLICE + piece * PIECE, PIECE), PIECE)
@@ -75,9 +83,10 @@
     for load in loads:
         load.start()
 
-    partners = [inner, mate]
+    partners = [inner, device(0, 1, 1), mate]
     partners += [device(dy, 0, fc) for dy in (1, -1, 2, -2) for fc in (0, 1)]
-    partners += [device(dy, 1, 0) for dy in (1, -1, 2, -2)]
+    partners += [device(dy, 1, z) for dy in (1, 2)]
+    partners += [device(dy, 1, 1 - z) for dy in (-1, -2)]
     barrier = pltpu.get_barrier_semaphore()
     for partner in partners:
         pl.semaphore_signal(barrier, inc=1, device_id=partner, device_id_type=MESH)
@@ -145,9 +154,8 @@
         own = own / jnp.sum(own, axis=1, keepdims=True)
         tokw[OWN, 0] = jnp.broadcast_to(own, (8, SEQ))
         for k, (blk, s) in enumerate(USED):
-            dy, flip_z = PLACES[blk]
             remote(
-                tokw.at[OWN, 0], tokw.at[blk, s], tokw_send.at[k], tokw_sem.at[blk, s], device(-dy, flip_z, s)
+                tokw.at[OWN, 0], tokw.at[blk, s], tokw_send.at[k], tokw_sem.at[blk, s], holder(blk, s)
             ).start()
 
     @pl.loop(0, SLOTS + 1)
@@ -232,7 +240,7 @@
         centre = x - jnp.mean(x, axis=-1, keepdims=True)
         spread = jnp.mean(centre * centre, axis=-1, keepdims=True)
         embedded = (centre * lax.rsqrt(spread + 1e-07) * params[1] + params[2]).astype(BF16)
-        embedded_out[0, rows, :] = embedded
+        emb[rows, :] = embedded
         values = embedded.astype(F32)
         unit = values * lax.rsqrt(jnp.sum(values * values, axis=-1, keepdims=True) + 1e-06)
 
@@ -245,6 +253,9 @@
         pass_on((OWN, 0), (M1, 0), q, up)
         pass_on((OWN, 0), (P1, 0), q, down)
         pass_on((OWN, 0), (OWN, 1), q, mate)
+
+    store = pltpu.make_async_copy(emb, embedded_out.at[0], store_sem)
+    store.start()
 
     for k in range(SLOTS):
         for s in range(PIECES):
@@ -307,15 +318,14 @@
             pass_on((M1, 0), (M2, 0), q, up)
             landed(slot(P1, 0, q), unit_sem.at[P1, 0, q])
             pass_on((P1, 0), (P2, 0), q, down)
-            pass_on((P1, 0), (C1, 0), q, inner)
+            pass_on((P1, 0), (C1, 0), q, across)
             pass_on((M1, 0), (M1, 1), q, mate)
-            pass_on((P1, 0), (P1, 1), q, mate)
 
         @pl.when(t >= CHUNKS)
         def _():
             q = t - CHUNKS
             landed(slot(P2, 0, q), unit_sem.at[P2, 0, q])
-            pass_on((P2, 0), (C2, 0), q, inner)
+            pass_on((P2, 0), (C2, 0), q, across)
             landed(slot(M2, 0, q), unit_sem.at[M2, 0, q])
             pass_on((M2, 0), (M2, 1), q, mate)
 
@@ -335,11 +345,9 @@
             sample = jnp.where((t == 4) | (t == 6), 1, 0)
             double(left, sample, jnp.where(t <= 4, OWN, P1), t >= 5)
 
-    all_landed(P1, 1)
-
     @pl.loop(0, 3)
     def _(t):
-        single(jnp.where(t < 2, OWN, P1), jnp.where(t < 2, t, z), C1)
+        single(jnp.where(t < 2, OWN, P1), t % 2, C1)
 
     all_landed(M2, 1)
     double(M2, 1, P1)
@@ -350,18 +358,18 @@
         def _():
             all_landed(C2, 0)
 
-        single(M2, jnp.where(t == 0, y // 4, z), P2 + t)
+        single(M2, jnp.where(t == 0, y // 4, 0), P2 + t)
 
     for k, (blk, s) in enumerate(USED):
-        dy, flip_z = PLACES[blk]
         remote(
-            result.at[blk, s], arrived.at[k], result_send.at[k], result_sem.at[k], device(dy, flip_z, s)
+            result.at[blk, s], arrived.at[k], result_send.at[k], result_sem.at[k], owner(blk, s)
         ).start()
     @pl.loop(0, CHUNKS)
     def _(q):
         for m, (src, _) in enumerate(moves):
             sent(slot(*src, q), unit_send.at[m, q])
 
+    store.wait()
     for k, (blk, s) in enumerate(USED):
         sent(result.at[blk, s], result_send.at[k])
     for k in range(len(USED)):
@@ -377,14 +385,42 @@
     scores_out[...] = jnp.where(line < 2, everything, jnp.where(line == 2, f_score, utility))
 
 
-def hand_out(embedded_ref, scores_ref, embedded_hbm, precision_ref, recall_ref, f_ref, utility_ref, sem):
-    copy = pltpu.make_async_copy(embedded_ref, embedded_hbm, sem)
-    copy.start()
-    precision_ref[...] = scores_ref[0:1, :32]
-    recall_ref[...] = scores_ref[1:2, :32]
-    f_ref[...] = scores_ref[2:3, :32]
-    utility_ref[...] = scores_ref[3:4, :1]
-    copy.wait()
+def hand_out(
+    embedded_ref, scores_ref, embedded_out, precision_out, recall_out, f_out, utility_out,
+    emb, scores, row_p, row_r, row_f, one, load_sem, store_sem, small_sem,
+):
+    parts = emb.shape[0]
+    rows = emb.shape[1]
+    loads = [
+        pltpu.make_async_copy(embedded_ref.at[0, pl.ds(k * rows, rows)], emb.at[k], load_sem.at[k])
+        for k in range(parts)
+    ]
+    stores = [
+        pltpu.make_async_copy(emb.at[k], embedded_out.at[0, pl.ds(k * rows, rows)], store_sem.at[k])
+        for k in range(parts)
+    ]
+    load_scores = pltpu.make_async_copy(scores_ref, scores, load_sem.at[parts])
+    load_scores.start()
+    for load in loads:
+        load.start()
+    load_scores.wait()
+    row_p[...] = scores[0:1, :32]
+    row_r[...] = scores[1:2, :32]
+    row_f[...] = scores[2:3, :32]
+    one[...] = scores[3:4, :1]
+    small = [
+        pltpu.make_async_copy(src, dst, small_sem.at[k])
+        for k, (src, dst) in enumerate(
+            ((row_p, precision_out), (row_r, recall_out), (row_f, f_out), (one, utility_out))
+        )
+    ]
+    for copy in small:
+        copy.start()
+    for load, store in zip(loads, stores):
+        load.wait()
+        store.start()
+    for copy in small + stores:
+        copy.wait()
 
 
 def local(
@@ -403,7 +439,7 @@
             jax.ShapeDtypeStruct((8, SEQ), F32),
         ),
         in_specs=[hbm] * 9,
-        out_specs=(vmem, vmem),
+        out_specs=(hbm, vmem),
         scratch_shapes=[
             pltpu.VMEM((2, SEQ, WIDTH), BF16),
             pltpu.VMEM((SEQ, WIDTH), BF16),
@@ -415,12 +451,14 @@
             pltpu.SMEM((1,), jnp.int32),
             pltpu.VMEM((vocab,), BF16),
             pltpu.VMEM((table_rows, SEQ), BF16),
+            pltpu.VMEM((SEQ, WIDTH), BF16),
             pltpu.VMEM((7, 2, SEQ, WIDTH), BF16),
             pltpu.VMEM((1, WIDTH), F32),
             pltpu.VMEM((7, 2, 8, SEQ), F32),
             pltpu.VMEM((7, 2, 8, SEQ), F32),
             pltpu.VMEM((count, 8, SEQ), F32),
             dma((8,)),
+            dma,
             dma((2, 2)),
             dma((SLOTS - 1, PIECES)),
             dma((SLOTS, PIECES)),
@@ -428,7 +466,7 @@
             dma,
             dma((SLOTS,)),
             dma((count,)),
-            dma((10, CHUNKS)),
+            dma((9, CHUNKS)),
             dma((count,)),
             dma((SLOTS, PIECES)),
             dma((SLOTS, PIECES)),
@@ -455,9 +493,20 @@
             jax.ShapeDtypeStruct((1, 32), F32),
             jax.ShapeDtypeStruct((1, 1), F32),
         ),
-        in_specs=[vmem, vmem],
-        out_specs=(pl.BlockSpec(memory_space=pl.ANY), vmem, vmem, vmem, vmem),
-        scratch_shapes=[dma],
+        in_specs=[hbm, hbm],
+        out_specs=(hbm,) * 5,
+        scratch_shapes=[
+            pltpu.VMEM((2, SEQ // 2, WIDTH), BF16),
+            pltpu.VMEM((8, SEQ), F32),
+            pltpu.VMEM((1, 32), F32),
+            pltpu.VMEM((1, 32), F32),
+            pltpu.VMEM((1, 32), F32),
+            pltpu.VMEM((1, 1), F32),
+            dma((3,)),
+            dma((2,)),
+            dma((4,)),
+        ],
+        compiler_params=pltpu.CompilerParams(vmem_limit_bytes=60 * 1024 * 1024),
     )(embedded, scores)
     return embedded, precision, recall, f_score, utility.reshape(1)
 

time: 52.3 us -> 51.6 us (0.987)
  Pallas kernels: 50.8 us -> 50.1 us
where the time goes in v3:
time: 51.6 us; the launch traced here: 51.4 us
  Pallas kernels  50.1 us (97%)
  between operations  1.29 us (2%)
    pallas_call x1, Pallas kernels, local(): pl.pallas_call(kernel, out_shape=(jax.ShapeDtypeStruct((1, SEQ, WIDTH), B...  48.4 us
    pallas_call x1, Pallas kernels, local(): pl.pallas_call(hand_out, out_shape=(jax.ShapeDtypeStruct((1, SEQ, WIDTH),...  1.71 us

profile of v3, /device:TPU:1, one launch (start us, length us, event | category | flops | bytes accessed | tf_op | source)
XLA Modules:
  0.0 51.4 jit_solution(15027602511242228086)
XLA Ops:
  1.3 48.4 %shard_map.128 = (bf16[1,128,1024]{2,1,0:T(8,128)(2,1)}, f32[8,128]{1,0:T(8,128)}) custom-call(bf16[1,128,1024]{2,1,0:T(8,128)(2,1)} %context_hbm.1, bf16[1,128,1024]{2,1,0:T(8,128)(2,1)} %hidden_hbm.1, bf16[32,1024]{1,0:T(8,128)(2,1)} %bitcast.5, f32[1,1024]{1,0:T(1,128)} %bitcast.6, f32[1,1024]{1,0:T(1,128)} %bitcast.7, f32[1,1024]{1,0:T(1,128)} %bitcast.8, ...), custom_call_target="tpu_custom_call" | custom-call | flops 1073741824 | bytes 1048576 | tf_op jit(solution)/shard_map/pallas_call | solution.py:435
  49.7 1.7 %shard_map.129 = (bf16[1,128,1024]{2,1,0:T(8,128)(2,1)}, f32[1,32]{1,0:T(1,128)}, f32[1,32]{1,0:T(1,128)}, f32[1,32]{1,0:T(1,128)}, f32[1,1]{1,0:T(1,128)}) custom-call(bf16[1,128,1024]{2,1,0:T(8,128)(2,1)} %get-tuple-element.12.embedded_ref, f32[8,128]{1,0:T(8,128)} %get-tuple-element.13.scores_ref), custom_call_target="tpu_custom_call" | custom-call | tf_op jit(solution)/shard_map/pallas_call | solution.py:487

commit v4 on v3

--- a/solution.py
+++ b/solution.py
@@ -61,6 +61,14 @@
 
     def rows_of(zz, piece):
         return pl.ds(pl.multiple_of(zz * 2 * SLICE + piece * PIECE, PIECE), PIECE)
+
+    partners = [inner, device(0, 1, 1), mate]
+    partners += [device(dy, 0, fc) for dy in (1, -1, 2, -2) for fc in (0, 1)]
+    partners += [device(dy, 1, z) for dy in (1, 2)]
+    partners += [device(dy, 1, 1 - z) for dy in (-1, -2)]
+    barrier = pltpu.get_barrier_semaphore()
+    for partner in partners:
+        pl.semaphore_signal(barrier, inc=1, device_id=partner, device_id_type=MESH)
 
     def own_piece(h):
         return weight_hbm.at[pl.ds(h * PIECE, PIECE)], wt.at[0, rows_of(z, c * 2 + h)]
@@ -82,14 +90,6 @@
     ]
     for load in loads:
         load.start()
-
-    partners = [inner, device(0, 1, 1), mate]
-    partners += [device(dy, 0, fc) for dy in (1, -1, 2, -2) for fc in (0, 1)]
-    partners += [device(dy, 1, z) for dy in (1, 2)]
-    partners += [device(dy, 1, 1 - z) for dy in (-1, -2)]
-    barrier = pltpu.get_barrier_semaphore()
-    for partner in partners:
-        pl.semaphore_signal(barrier, inc=1, device_id=partner, device_id_type=MESH)
 
     def remote(src, dst, send_sem, recv_sem, target):
         return pltpu.make_async_remote_copy(
@@ -153,6 +153,8 @@
         own = jnp.where(lane < length_ref[0], found, 0.0)
         own = own / jnp.sum(own, axis=1, keepdims=True)
         tokw[OWN, 0] = jnp.broadcast_to(own, (8, SEQ))
+
+    def send_token_weights():
         for k, (blk, s) in enumerate(USED):
             remote(
                 tokw.at[OWN, 0], tokw.at[blk, s], tokw_send.at[k], tokw_sem.at[blk, s], holder(blk, s)
@@ -211,9 +213,13 @@
                 ).start()
                 mixed[:, at] = both[:SEQ, side]
 
-        @pl.when(k == 3)
+        @pl.when(k == 0)
         def _():
             token_weights()
+
+        @pl.when(k == 1)
+        def _():
+            send_token_weights()
 
     for load in loads[4:]:
         load.wait()
@@ -267,8 +273,9 @@
                 sent(wt.at[k, rows_of(z, s)], z_send.at[k, s])
         sent(part.at[k], part_send.at[k])
     sent(ctx.at[0], ctx_send)
-    for k in range(len(USED)):
+    for k, (blk, s) in enumerate(USED):
         sent(tokw.at[OWN, 0], tokw_send.at[k])
+        landed(tokw.at[blk, s], tokw_sem.at[blk, s])
     for h in (0, 1):
         sent(own_piece(h)[0], first_sem.at[1, h])
 
@@ -328,11 +335,6 @@
             pass_on((P2, 0), (C2, 0), q, across)
             landed(slot(M2, 0, q), unit_sem.at[M2, 0, q])
             pass_on((M2, 0), (M2, 1), q, mate)
-
-        @pl.when(t == 2)
-        def _():
-            for blk, s in USED:
-                landed(tokw.at[blk, s], tokw_sem.at[blk, s])
 
         for when, blk, s in ((4, OWN, 1), (5, C1, 0), (6, M1, 1)):
             @pl.when(t == when)

time: 51.6 us -> 52.2 us (1.012)
  Pallas kernels: 50.1 us -> 50.7 us
    pallas_call x1, Pallas kernels: 48.4 us -> 49 us  [local(): pl.pallas_call(kernel, out_shape=(jax.ShapeDtypeStruct((1, SEQ, WIDTH), B...]
where the time goes in v4:
time: 52.2 us; the launch traced here: 52 us
  Pallas kernels  50.7 us (97%)
  between operations  1.29 us (2%)
    pallas_call x1, Pallas kernels, local(): pl.pallas_call(kernel, out_shape=(jax.ShapeDtypeStruct((1, SEQ, WIDTH), B...  49 us
    pallas_call x1, Pallas kernels, local(): pl.pallas_call(hand_out, out_shape=(jax.ShapeDtypeStruct((1, SEQ, WIDTH),...  1.71 us

profile of v4, /device:TPU:1, one launch (start us, length us, event | category | flops | bytes accessed | tf_op | source)
XLA Modules:
  0.0 52.0 jit_solution(5740297547383078731)
XLA Ops:
  1.3 49.0 %shard_map.128 = (bf16[1,128,1024]{2,1,0:T(8,128)(2,1)}, f32[8,128]{1,0:T(8,128)}) custom-call(bf16[1,128,1024]{2,1,0:T(8,128)(2,1)} %context_hbm.1, bf16[1,128,1024]{2,1,0:T(8,128)(2,1)} %hidden_hbm.1, bf16[32,1024]{1,0:T(8,128)(2,1)} %bitcast.5, f32[1,1024]{1,0:T(1,128)} %bitcast.6, f32[1,1024]{1,0:T(1,128)} %bitcast.7, f32[1,1024]{1,0:T(1,128)} %bitcast.8, ...), custom_call_target="tpu_custom_call" | custom-call | flops 1073741824 | bytes 1048576 | tf_op jit(solution)/shard_map/pallas_call | solution.py:437
  50.3 1.7 %shard_map.129 = (bf16[1,128,1024]{2,1,0:T(8,128)(2,1)}, f32[1,32]{1,0:T(1,128)}, f32[1,32]{1,0:T(1,128)}, f32[1,32]{1,0:T(1,128)}, f32[1,1]{1,0:T(1,128)}) custom-call(bf16[1,128,1024]{2,1,0:T(8,128)(2,1)} %get-tuple-element.12.embedded_ref, f32[8,128]{1,0:T(8,128)} %get-tuple-element.13.scores_ref), custom_call_target="tpu_custom_call" | custom-call | tf_op jit(solution)/shard_map/pallas_call | solution.py:489

commit v5 on v3

--- a/solution.py
+++ b/solution.py
@@ -198,18 +198,17 @@
             for n in (0, 1):
                 for s in range(PIECES // 2):
                     landed(wt.at[first + n, rows_of(1 - z, s)], z_sem.at[first + n, s])
-            both = lax.dot_general(
-                ctx[...].reshape(2 * SEQ, WIDTH), wt[pl.ds(first, 2)].reshape(2 * SEQ, WIDTH), NT,
-                preferred_element_type=F32,
-            )
+            columns = wt[pl.ds(first, 2)].reshape(2 * SEQ, WIDTH)
+            theirs = lax.dot_general(ctx[1], columns, NT, preferred_element_type=F32)
             for n in (0, 1):
-                at = columns_at(first + n, c)
-                side = slice(n * SEQ, (n + 1) * SEQ)
-                part[first + n] = both[SEQ:, side]
+                part[first + n] = theirs[:, n * SEQ:(n + 1) * SEQ]
                 remote(
-                    part.at[first + n], mixed.at[:, at], part_send.at[first + n], part_sem.at[first + n], mate
+                    part.at[first + n], mixed.at[:, columns_at(first + n, c)], part_send.at[first + n],
+                    part_sem.at[first + n], mate,
                 ).start()
-                mixed[:, at] = both[:SEQ, side]
+            mine = lax.dot_general(ctx[0], columns, NT, preferred_element_type=F32)
+            for n in (0, 1):
+                mixed[:, columns_at(first + n, c)] = mine[:, n * SEQ:(n + 1) * SEQ]
 
         @pl.when(k == 3)
         def _():
@@ -352,23 +351,25 @@
     all_landed(M2, 1)
     double(M2, 1, P1)
 
-    @pl.loop(0, 2)
-    def _(t):
-        @pl.when(t == 1)
-        def _():
-            all_landed(C2, 0)
-
-        single(M2, jnp.where(t == 0, y // 4, 0), P2 + t)
-
-    for k, (blk, s) in enumerate(USED):
-        remote(
-            result.at[blk, s], arrived.at[k], result_send.at[k], result_sem.at[k], owner(blk, s)
-        ).start()
+    single(M2, y // 4, P2)
+
+    def send_results(blocks):
+        for k, (blk, s) in enumerate(USED):
+            if blk in blocks:
+                remote(
+                    result.at[blk, s], arrived.at[k], result_send.at[k], result_sem.at[k], owner(blk, s)
+                ).start()
+
+    send_results((OWN, M1, P1, C1))
+
     @pl.loop(0, CHUNKS)
     def _(q):
         for m, (src, _) in enumerate(moves):
             sent(slot(*src, q), unit_send.at[m, q])
 
+    all_landed(C2, 0)
+    single(M2, 0, C2)
+    send_results((M2, P2, C2))
     store.wait()
     for k, (blk, s) in enumerate(USED):
         sent(result.at[blk, s], result_send.at[k])

time: 51.6 us -> 51.8 us (level)
  no operation moved by 1% of the time
where the time goes in v5:
time: 51.8 us; the launch traced here: 51.6 us
  Pallas kernels  50.4 us (97%)
  between operations  1.29 us (2%)
    pallas_call x1, Pallas kernels, local(): pl.pallas_call(kernel, out_shape=(jax.ShapeDtypeStruct((1, SEQ, WIDTH), B...  48.6 us
    pallas_call x1, Pallas kernels, local(): pl.pallas_call(hand_out, out_shape=(jax.ShapeDtypeStruct((1, SEQ, WIDTH),...  1.71 us

profile of v5, /device:TPU:1, one launch (start us, length us, event | category | flops | bytes accessed | tf_op | source)
XLA Modules:
  0.0 51.6 jit_solution(9463733430333638012)
XLA Ops:
  1.3 48.6 %shard_map.128 = (bf16[1,128,1024]{2,1,0:T(8,128)(2,1)}, f32[8,128]{1,0:T(8,128)}) custom-call(bf16[1,128,1024]{2,1,0:T(8,128)(2,1)} %context_hbm.1, bf16[1,128,1024]{2,1,0:T(8,128)(2,1)} %hidden_hbm.1, bf16[32,1024]{1,0:T(8,128)(2,1)} %bitcast.5, f32[1,1024]{1,0:T(1,128)} %bitcast.6, f32[1,1024]{1,0:T(1,128)} %bitcast.7, f32[1,1024]{1,0:T(1,128)} %bitcast.8, ...), custom_call_target="tpu_custom_call" | custom-call | flops 1073741824 | bytes 1048576 | tf_op jit(solution)/shard_map/pallas_call | solution.py:436
  49.9 1.7 %shard_map.129 = (bf16[1,128,1024]{2,1,0:T(8,128)(2,1)}, f32[1,32]{1,0:T(1,128)}, f32[1,32]{1,0:T(1,128)}, f32[1,32]{1,0:T(1,128)}, f32[1,1]{1,0:T(1,128)}) custom-call(bf16[1,128,1024]{2,1,0:T(8,128)(2,1)} %get-tuple-element.12.embedded_ref, f32[8,128]{1,0:T(8,128)} %get-tuple-element.13.scores_ref), custom_call_target="tpu_custom_call" | custom-call | tf_op jit(solution)/shard_map/pallas_call | solution.py:488

commit v6 on v5

--- a/solution.py
+++ b/solution.py
@@ -172,7 +172,7 @@
                         wt.at[k, rows], wt.at[k + 1, rows], chain_send.at[k, s], slice_sem.at[k + 1, s], ahead
                     ).start()
 
-                @pl.when((k == 0) | (s < PIECES // 2))
+                @pl.when((k == 0) | (s < PIECES // 2) | ((k == 3) & (c == 1)))
                 def _(rows=rows, s=s):
                     remote(wt.at[k, rows], wt.at[k, rows], z_send.at[k, s], z_sem.at[k, s], inner).start()
 
@@ -182,7 +182,7 @@
                 rows = rows_of(1 - z, s)
                 landed(wt.at[k - 1, rows], z_sem.at[k - 1, s])
 
-                @pl.when(k < SLOTS)
+                @pl.when((k < 3) | ((k == 3) & (c == 0)))
                 def _(rows=rows, s=s):
                     remote(
                         wt.at[k - 1, rows], wt.at[k, rows], side_send.at[k - 1, s - PIECES // 2], z_sem.at[k, s], ahead
@@ -260,7 +260,15 @@
         for s in range(PIECES):
             if k + 1 < SLOTS:
                 sent(wt.at[k, rows_of(z, s)], chain_send.at[k, s])
-                if s >= PIECES // 2:
+                if k == 2 and s >= PIECES // 2:
+                    @pl.when(c == 0)
+                    def _(s=s):
+                        sent(wt.at[2, rows_of(1 - z, s)], side_send.at[2, s - PIECES // 2])
+
+                    @pl.when(c == 1)
+                    def _(s=s):
+                        sent(wt.at[3, rows_of(z, s)], z_send.at[3, s])
+                elif s >= PIECES // 2:
                     sent(wt.at[k, rows_of(1 - z, s)], side_send.at[k, s - PIECES // 2])
             if k == 0 or s < PIECES // 2:
                 sent(wt.at[k, rows_of(z, s)], z_send.at[k, s])

time: 51.8 us -> 51.6 us (level)
  no operation moved by 1% of the time
where the time goes in v6:
time: 51.6 us; the launch traced here: 51.5 us
  Pallas kernels  50.2 us (97%)
  between operations  1.29 us (2%)
    pallas_call x1, Pallas kernels, local(): pl.pallas_call(kernel, out_shape=(jax.ShapeDtypeStruct((1, SEQ, WIDTH), B...  48.5 us
    pallas_call x1, Pallas kernels, local(): pl.pallas_call(hand_out, out_shape=(jax.ShapeDtypeStruct((1, SEQ, WIDTH),...  1.71 us

profile of v6, /device:TPU:1, one launch (start us, length us, event | category | flops | bytes accessed | tf_op | source)
XLA Modules:
  0.0 51.5 jit_solution(13513273763642670292)
XLA Ops:
  1.3 48.5 %shard_map.128 = (bf16[1,128,1024]{2,1,0:T(8,128)(2,1)}, f32[8,128]{1,0:T(8,128)}) custom-call(bf16[1,128,1024]{2,1,0:T(8,128)(2,1)} %context_hbm.1, bf16[1,128,1024]{2,1,0:T(8,128)(2,1)} %hidden_hbm.1, bf16[32,1024]{1,0:T(8,128)(2,1)} %bitcast.5, f32[1,1024]{1,0:T(1,128)} %bitcast.6, f32[1,1024]{1,0:T(1,128)} %bitcast.7, f32[1,1024]{1,0:T(1,128)} %bitcast.8, ...), custom_call_target="tpu_custom_call" | custom-call | flops 1073741824 | bytes 1048576 | tf_op jit(solution)/shard_map/pallas_call | solution.py:444
  49.8 1.7 %shard_map.129 = (bf16[1,128,1024]{2,1,0:T(8,128)(2,1)}, f32[1,32]{1,0:T(1,128)}, f32[1,32]{1,0:T(1,128)}, f32[1,32]{1,0:T(1,128)}, f32[1,1]{1,0:T(1,128)}) custom-call(bf16[1,128,1024]{2,1,0:T(8,128)(2,1)} %get-tuple-element.12.embedded_ref, f32[8,128]{1,0:T(8,128)} %get-tuple-element.13.scores_ref), custom_call_target="tpu_custom_call" | custom-call | tf_op jit(solution)/shard_map/pallas_call | solution.py:496
